TPU v7x, 32 devices: a whole 2x2x4 slice. The times are simulated.
32 devices in a mesh: view: 4 (over y, x), tile: 8 (over z, core).
Axes of the slice: x: 2, y: 2, z: 4, core: 2. Of those that a mesh axis runs over, the one named last changes fastest.
Arguments:
- latents: bfloat16 [16, 2048, 1536], P('view', 'tile'), may hold values from -14 to 14
- qkv_weight: bfloat16 [1536, 3072], replicated, may hold values from -0.15625 to 0.15625
- out_weight: bfloat16 [1024, 1536], replicated, may hold values from -0.1875 to 0.1875
- anchor: int32 [1], replicated, may hold values from 0 to 15
- epi_list: int32 [16, 16, 6], P('view'), may hold values from -1 to 31, as said below
Outputs:
- attn_out: bfloat16 [16, 2048, 1536], P('view', 'tile')
Inputs may be any that keep to these rules, and one draw needn't show every extreme that they name: `epi_list`: row (v, b) lists distinct key blocks: an id c < 16 is block c of view (v - 1) mod 16, an id c >= 16 is block c - 16 of view (v + 1) mod 16; unused slots hold -1 and follow the used ones. Every row uses 1 to 6 slots, with a cap that varies from view to view, and some row uses all 6.
All inputs are finite; a program needn't handle non-finite values.
Results may differ from a plain program's by a relative error of at most 0.005.
The roundings to bfloat16 on the way count: a program that leaves them out, or rounds other values in their place, can miss the bound.
Values may be sent and summed in bfloat16 or wider, within the bound.
A program may use at most 128 MiB of HBM per device.

v0:
```python
import math

import jax
import jax.numpy as jnp
from jax import lax
from jax.sharding import PartitionSpec as P

HEADS = 8
HD = 128
VT = 2048
BLK = 128
NBLK = 16


def spread_2(array, axis, root):
    mine = lax.axis_index(axis) == root
    return lax.psum(jnp.where(mine, array, jnp.zeros_like(array)), axis)


def from_behind(array, axis, by):
    count = lax.axis_size(axis)
    return lax.ppermute(array, axis, [(i, (i + by) % count) for i in range(count)])


def allowed_tokens(epi_rows):
    blocks = jnp.any(
        epi_rows[:, :, None] == jnp.arange(2 * NBLK, dtype=jnp.int32)[None, None, :], axis=1
    )
    nearby = jnp.repeat(jnp.repeat(blocks, BLK, axis=0), BLK, axis=1)
    always = jnp.ones((VT, VT), dtype=bool)
    return jnp.concatenate([always, nearby, always], axis=1)


def attend(queries, keys_part, values_part, allowed):
    scores = jnp.einsum(
        "qd,kd->qk", queries, keys_part, preferred_element_type=jnp.float32
    ) / math.sqrt(HD)
    scores = jnp.where(allowed, scores, -jnp.inf)
    row_peak = jnp.max(scores, axis=1, keepdims=True)
    raised = jnp.exp(scores - row_peak)
    row_total = jnp.sum(raised, axis=1, keepdims=True)
    weights = raised.astype(jnp.bfloat16)
    summed = jnp.einsum("qk,kd->qd", weights, values_part, preferred_element_type=jnp.float32)
    return (summed / row_total).astype(jnp.bfloat16)


def body(latents, qkv_weight, out_weight, anchor, epi_list):
    per_dev, tile_tokens, model_width = latents.shape
    tile_count = lax.axis_size("tile")
    view_tokens = tile_tokens * tile_count
    parts = max(1, tile_count // (per_dev * HEADS))
    units = per_dev * HEADS * parts // tile_count
    part_rows = view_tokens // parts
    per_view = tile_count // per_dev
    shaped = qkv_weight.reshape(model_width, HEADS, 3 * HD)
    projected = jnp.einsum(
        "vtd,dhc->vhtc", latents, shaped, preferred_element_type=jnp.float32
    ).astype(jnp.bfloat16)
    key_values = projected[..., HD:]

    def spread(source):
        wide = jnp.broadcast_to(source[:, :, None], (per_dev, HEADS, parts) + source.shape[2:])
        return wide.reshape(tile_count, units, tile_tokens, source.shape[-1])

    target = anchor[0]
    anchor_tile = lax.dynamic_index_in_dim(key_values, target % per_dev, 0, keepdims=False)
    anchor_tile = spread_2(anchor_tile, "view", target // per_dev)
    anchor_send = spread(jnp.broadcast_to(anchor_tile[None], key_values.shape))
    boundary = [
        from_behind(key_values[per_dev - 1 if offset == 1 else 0], "view", offset)
        for offset in (1, -1)
    ]
    earlier = jnp.concatenate([boundary[0][None], key_values[:-1]], axis=0)
    following = jnp.concatenate([key_values[1:], boundary[1][None]], axis=0)
    resident, anchored, earlier, following = (
        lax.all_to_all(spread(projected), "tile", split_axis=0, concat_axis=2, tiled=True),
        lax.all_to_all(anchor_send, "tile", split_axis=0, concat_axis=2, tiled=True),
        lax.all_to_all(spread(earlier), "tile", split_axis=0, concat_axis=2, tiled=True),
        lax.all_to_all(spread(following), "tile", split_axis=0, concat_axis=2, tiled=True),
    )
    resident, anchored, earlier, following = (resident[0], anchored[0], earlier[0], following[0])
    tile_index = lax.axis_index("tile")
    local_view = tile_index // per_view
    epi_rows = lax.dynamic_index_in_dim(epi_list, local_view, 0, keepdims=False)
    allowed = allowed_tokens(epi_rows)
    joined = jnp.concatenate([resident[..., HD:], earlier, following, anchored], axis=1)
    block_rows = min(512, part_rows)
    block_count = part_rows // block_rows
    part_ids = (tile_index * units + jnp.arange(units, dtype=jnp.int32)) % parts

    def one_unit(unit_items):
        all_queries, keyvals, part_id = unit_items
        start = part_id * part_rows
        queries = lax.dynamic_slice_in_dim(all_queries, start, part_rows, 0).reshape(
            block_count, block_rows, HD
        )
        mask_rows = lax.dynamic_slice_in_dim(allowed, start, part_rows, 0).reshape(
            block_count, block_rows, 4 * view_tokens
        )

        def one_block(block_items):
            query_rows, block_mask = block_items
            return attend(query_rows, keyvals[:, :HD], keyvals[:, HD:], block_mask)

        return lax.map(one_block, (queries, mask_rows)).reshape(part_rows, HD)

    attended = lax.map(one_unit, (resident[..., :HD], joined, part_ids))
    pieces = attended.reshape(units, tile_count // parts, tile_tokens, HD).transpose(1, 0, 2, 3)
    selected = part_ids[None, :] == jnp.arange(parts, dtype=jnp.int32)[:, None]
    outgoing = jnp.where(
        selected[:, None, :, None, None], pieces[None], jnp.zeros((), jnp.bfloat16)
    )
    outgoing = outgoing.reshape(tile_count, units, tile_tokens, HD)
    returned = lax.all_to_all(outgoing, "tile", split_axis=0, concat_axis=1, tiled=True).reshape(
        per_dev, HEADS, parts, tile_tokens, HD
    )
    own_part = tile_index // (tile_count // parts)
    returned = lax.dynamic_index_in_dim(returned, own_part, 2, keepdims=False)
    projected_out = jnp.einsum(
        "vhtc,hcd->vtd",
        returned,
        out_weight.reshape(HEADS, HD, model_width),
        preferred_element_type=jnp.float32,
    )
    return projected_out.astype(jnp.bfloat16)


def solution(mesh):
    return jax.shard_map(
        body,
        mesh=mesh,
        in_specs=(P("view", "tile", None), P(), P(), P(), P("view", None, None)),
        out_specs=P("view", "tile", None),
        check_vma=False,
    )
```

profile of v0, /device:TPU:0, one launch (start us, length us, event | category | flops | bytes accessed | tf_op | source)
XLA Modules:
  0.0 1073.6 jit_solution(12551528584751973649)
XLA Ops:
  7.4 12.9 %copy.52 = bf16[1536,3072]{0,1:T(8,128)(2,1)} copy(bf16[1536,3072]{1,0:T(8,128)(2,1)} %param.10) | data formatting | bytes 18874368 | tf_op jit(solution)/shard_map/reshape | solution.py:55
  20.2 12.6 %convert_bitcast_fusion = bf16[4,8,256,384]{2,3,0,1:T(8,128)(2,1)S(1)} fusion(bf16[1536,8,384,1]{0,2,3,1:T(8,128)(2,1)} %bitcast.117, bf16[4,256,1536]{2,1,0:T(8,128)(2,1)S(1)} %copy-done), kind=kOutput, calls=%fused_computation.22 | convolution fusion | flops 9666822144 | bytes 18874368 | tf_op jit(solution)/shard_map/vtd,dhc->vhtc/dot_general | solution.py:56
  40.2 55.4 %all-reduce.2.cloned.1.call-done = bf16[8,256,256]{1,2,0:T(8,128)(2,1)} async-done(((bf16[8,256,256]{1,2,0:T(8,128)(2,1)}), bf16[8,256,256]{1,2,0:T(8,128)(2,1)}) %all-reduce.2.cloned.1.call-update) | async-done | bytes 1048592 | tf_op jit(solution)/shard_map/psum | solution.py:17
  112.4 20.5 %collective-permute-done = bf16[8,256,256]{1,2,0:T(8,128)(2,1)S(1)} collective-permute-done((bf16[8,256,256]{1,2,0:T(8,128)(2,1)S(1)}, bf16[8,256,256]{1,2,0:T(8,128)(2,1)S(1)}, u32[]{:S(2)}, u32[]{:S(2)}) %collective-permute-start) | collective-permute-done | bytes 1048608 | tf_op jit(solution)/shard_map/ppermute | solution.py:22
  132.9 22.0 %collective-permute-done.1 = bf16[8,256,256]{1,2,0:T(8,128)(2,1)S(1)} collective-permute-done((bf16[8,256,256]{1,2,0:T(8,128)(2,1)S(1)}, bf16[8,256,256]{1,2,0:T(8,128)(2,1)S(1)}, u32[]{:S(2)}, u32[]{:S(2)}) %collective-permute-start.1) | collective-permute-done | bytes 1048608 | tf_op jit(solution)/shard_map/ppermute | solution.py:22
  164.7 33.7 %all-to-all-done.3 = bf16[8,4,256,256]{3,2,1,0:T(8,128)(2,1)} async-done(((bf16[8,4,256,256]{3,2,1,0:T(8,128)(2,1)}), bf16[8,4,256,256]{3,2,1,0:T(8,128)(2,1)}, u32[]{:S(2)}, u32[]{:S(2)}) %all-to-all-start.3) | async-done | bytes 4194336 | tf_op jit(solution)/shard_map/all_to_all | solution.py:77
  209.2 87.8 %all-to-all-done.1 = bf16[8,4,256,256]{3,2,1,0:T(8,128)(2,1)} async-done(((bf16[8,4,256,256]{3,2,1,0:T(8,128)(2,1)}), bf16[8,4,256,256]{3,2,1,0:T(8,128)(2,1)}, u32[]{:S(2)}, u32[]{:S(2)}) %all-to-all-start.1) | async-done | bytes 4194336 | tf_op jit(solution)/shard_map/all_to_all | solution.py:78
  310.2 85.3 %all-to-all-done.2 = bf16[8,4,256,256]{3,2,1,0:T(8,128)(2,1)} async-done(((bf16[8,4,256,256]{3,2,1,0:T(8,128)(2,1)}), bf16[8,4,256,256]{3,2,1,0:T(8,128)(2,1)}, u32[]{:S(2)}, u32[]{:S(2)}) %all-to-all-start.2) | async-done | bytes 4194336 | tf_op jit(solution)/shard_map/all_to_all | solution.py:79
  401.4 11.2 %broadcast_in_dim.53 = pred[2048,32,128]{2,1,0:T(8,128)(4,1)S(1)} broadcast(pred[2048,32]{1,0:T(8,128)(4,1)S(1)} %bitcast.123), dimensions={0,1} | broadcast | bytes 8454144 | tf_op jit(solution)/shard_map/broadcast_in_dim | solution.py:29
  421.2 9.1 pad_add_fusion
  444.1 95.2 %all-to-all-done = bf16[8,4,256,384]{3,2,1,0:T(8,128)(2,1)} async-done(((bf16[8,4,256,384]{3,2,1,0:T(8,128)(2,1)}), bf16[8,4,256,384]{3,2,1,0:T(8,128)(2,1)}, u32[]{:S(2)}, u32[]{:S(2)}) %all-to-all-start) | async-done | bytes 6291488 | tf_op jit(solution)/shard_map/all_to_all | solution.py:76
  555.2 453.1 %while.25 = (s32[]{:T(128)}, bf16[4,2048,128]{2,1,0:T(8,128)(2,1)}, bf16[4,2048,128]{2,1,0:T(8,128)(2,1)}, pred[2048,8192]{1,0:T(32,128)(4,1)}, bf16[4,8192,256]...) while((s32[]{:T(128)}, bf16[4,2048,128]{2,1,0:T(8,128)(2,1)}, bf16[4,2048,128]{2,1,0:T(8,128)(2,1)}, ...), condition=%wide.region_7.8_spmd, body=%wide.region_2.7_spmd.sunk | while | flops 2176973824 | bytes 69480664 | solution.py:107
  560.8 106.8 %while.26 = (s32[]{:T(128)}, bf16[4,512,128]{2,1,0:T(8,128)(2,1)S(1)}, pred[4,512,8192]{2,1,0:T(32,128)(4,1)}, bf16[4,512,128]{2,1,0:T(8,128)(2,1)S(1)}, bf16[8192,256]{1,0:T(8,128)(2,1)}, /*index=5*/s32[]{:T(128)}) while((s32[]{:T(128)}, bf16[4,512,128]{2,1,0:T(8,128)(2,1)S(1)}, pred[4,512,8192]{2,1,0:T(32,128)(4,1)}, ...), condition=%wide.region_6.6_spmd, body=%wide.region_3.5_spmd.sunk | while | flops 2176973824 | bytes 58994244 | solution.py:105
  560.8 9.8 fusion.44
  578.7 8.8 fusion.46
  587.5 9.8 fusion.44
  605.4 8.8 fusion.46
  614.3 9.8 fusion.44
  632.1 8.8 fusion.46
  641.0 9.8 fusion.44
  658.9 8.8 fusion.46
  674.1 106.8 %while.26 = (s32[]{:T(128)}, bf16[4,512,128]{2,1,0:T(8,128)(2,1)S(1)}, pred[4,512,8192]{2,1,0:T(32,128)(4,1)}, bf16[4,512,128]{2,1,0:T(8,128)(2,1)S(1)}, bf16[8192,256]{1,0:T(8,128)(2,1)}, /*index=5*/s32[]{:T(128)}) while((s32[]{:T(128)}, bf16[4,512,128]{2,1,0:T(8,128)(2,1)S(1)}, pred[4,512,8192]{2,1,0:T(32,128)(4,1)}, ...), condition=%wide.region_6.6_spmd, body=%wide.region_3.5_spmd.sunk | while | flops 2176973824 | bytes 58994244 | solution.py:105
  674.1 9.8 fusion.44
  692.0 8.8 fusion.46
  700.8 9.8 fusion.44
  718.7 8.8 fusion.46
  727.5 9.8 fusion.44
  745.4 8.8 fusion.46
  754.2 9.8 fusion.44
  772.1 8.8 fusion.46
  787.4 106.8 %while.26 = (s32[]{:T(128)}, bf16[4,512,128]{2,1,0:T(8,128)(2,1)S(1)}, pred[4,512,8192]{2,1,0:T(32,128)(4,1)}, bf16[4,512,128]{2,1,0:T(8,128)(2,1)S(1)}, bf16[8192,256]{1,0:T(8,128)(2,1)}, /*index=5*/s32[]{:T(128)}) while((s32[]{:T(128)}, bf16[4,512,128]{2,1,0:T(8,128)(2,1)S(1)}, pred[4,512,8192]{2,1,0:T(32,128)(4,1)}, ...), condition=%wide.region_6.6_spmd, body=%wide.region_3.5_spmd.sunk | while | flops 2176973824 | bytes 58994244 | solution.py:105
  787.4 9.8 fusion.44
  805.3 8.8 fusion.46
  814.1 9.8 fusion.44
  832.0 8.8 fusion.46
  840.8 9.8 fusion.44
  858.7 8.8 fusion.46
  867.5 9.8 fusion.44
  885.4 8.8 fusion.46
  900.7 106.8 %while.26 = (s32[]{:T(128)}, bf16[4,512,128]{2,1,0:T(8,128)(2,1)S(1)}, pred[4,512,8192]{2,1,0:T(32,128)(4,1)}, bf16[4,512,128]{2,1,0:T(8,128)(2,1)S(1)}, bf16[8192,256]{1,0:T(8,128)(2,1)}, /*index=5*/s32[]{:T(128)}) while((s32[]{:T(128)}, bf16[4,512,128]{2,1,0:T(8,128)(2,1)S(1)}, pred[4,512,8192]{2,1,0:T(32,128)(4,1)}, ...), condition=%wide.region_6.6_spmd, body=%wide.region_3.5_spmd.sunk | while | flops 2176973824 | bytes 58994244 | solution.py:105
  900.7 9.8 fusion.44
  918.6 8.8 fusion.46
  927.4 9.8 fusion.44
  945.3 8.8 fusion.46
  954.1 9.8 fusion.44
  972.0 8.8 fusion.46
  980.8 9.8 fusion.44
  1010.3 51.5 %all_to_all.69 = bf16[8,4,256,128]{3,2,1,0:T(8,128)(2,1)S(1)} all-to-all(bf16[8,4,256,128]{3,2,1,0:T(8,128)(2,1)S(1)} %bitcast.118), channel_id=1, replica_groups=mesh['view'=4,'tile'=8] {'tile'}, dimensions={0} | all-to-all | bytes 4194304 | tf_op jit(solution)/shard_map/all_to_all | solution.py:114
  (81 shorter events, 273.1 us)
Async XLA Ops:
  6.5 13.7 %copy-start = (bf16[4,256,1536]{2,1,0:T(8,128)(2,1)S(1)}, bf16[4,256,1536]{2,1,0:T(8,128)(2,1)}, u32[]{:S(2)}) copy-start(bf16[4,256,1536]{2,1,0:T(8,128)(2,1)} %param.9) | copy-start | bytes 9437188
  6.5 89.1 %all-reduce.2.cloned.1.call-start = ((), (), s32[]{:S(2)}) async-start(), calls=%async_computation.5 | async-start | bytes 2097152 | tf_op jit(solution)/shard_map/psum | solution.py:17
  32.8 2.6 copy-start.2
  99.7 98.7 %all-to-all-start.3 = ((bf16[8,4,256,256]{3,2,1,0:T(8,128)(2,1)}), bf16[8,4,256,256]{3,2,1,0:T(8,128)(2,1)}, u32[]{:S(2)}, u32[]{:S(2)}) async-start(bf16[8,4,256,256]{3,2,1,0:T(8,128)(2,1)} %bitcast.110), calls=%async_computation.3 | async-start | bytes 8388608 | tf_op jit(solution)/shard_map/all_to_all | solution.py:77
  106.0 26.9 %collective-permute-start = (bf16[8,256,256]{1,2,0:T(8,128)(2,1)S(1)}, bf16[8,256,256]{1,2,0:T(8,128)(2,1)S(1)}, u32[]{:S(2)}, u32[]{:S(2)}) collective-permute-start(bf16[8,256,256]{1,2,0:T(8,128)(2,1)S(1)} %get-tuple-element.96), channel_id=1, source_target_pairs={{0,8},{8,16},{16,24},{24,0},{1,9},{9,17},{17,25},{25,1},{2,10},{10... | collective-permute-start | bytes 3145736 | tf_op jit(solution)/shard_map/ppermute | solution.py:22
  107.5 47.4 %collective-permute-start.1 = (bf16[8,256,256]{1,2,0:T(8,128)(2,1)S(1)}, bf16[8,256,256]{1,2,0:T(8,128)(2,1)S(1)}, u32[]{:S(2)}, u32[]{:S(2)}) collective-permute-start(bf16[8,256,256]{1,2,0:T(8,128)(2,1)S(1)} %get-tuple-element.97), channel_id=1, source_target_pairs={{0,24},{8,0},{16,8},{24,16},{1,25},{9,1},{17,9},{25,17},{2,26},{10... | collective-permute-start | bytes 3145736 | tf_op jit(solution)/shard_map/ppermute | solution.py:22
  198.4 98.6 %all-to-all-start.1 = ((bf16[8,4,256,256]{3,2,1,0:T(8,128)(2,1)}), bf16[8,4,256,256]{3,2,1,0:T(8,128)(2,1)}, u32[]{:S(2)}, u32[]{:S(2)}) async-start(bf16[8,4,256,256]{3,2,1,0:T(8,128)(2,1)} %bitcast.111), calls=%async_computation.1 | async-start | bytes 8388608 | tf_op jit(solution)/shard_map/all_to_all | solution.py:78
  297.0 98.6 %all-to-all-start.2 = ((bf16[8,4,256,256]{3,2,1,0:T(8,128)(2,1)}), bf16[8,4,256,256]{3,2,1,0:T(8,128)(2,1)}, u32[]{:S(2)}, u32[]{:S(2)}) async-start(bf16[8,4,256,256]{3,2,1,0:T(8,128)(2,1)} %bitcast.112), calls=%async_computation.2 | async-start | bytes 8388608 | tf_op jit(solution)/shard_map/all_to_all | solution.py:79
  395.5 143.7 %all-to-all-start = ((bf16[8,4,256,384]{3,2,1,0:T(8,128)(2,1)}), bf16[8,4,256,384]{3,2,1,0:T(8,128)(2,1)}, u32[]{:S(2)}, u32[]{:S(2)}) async-start(bf16[8,4,256,384]{3,2,1,0:T(8,128)(2,1)} %bitcast.107), calls=%async_computation | async-start | bytes 12582912 | tf_op jit(solution)/shard_map/all_to_all | solution.py:76
  542.9 2.9 copy-start.4
  542.9 4.2 copy-start.5
  543.2 5.2 copy-start.3
  1008.3 53.5 %copy-start.6 = (bf16[1024,1536]{1,0:T(8,128)(2,1)S(1)}, bf16[1024,1536]{1,0:T(8,128)(2,1)}, u32[]{:S(2)}) copy-start(bf16[1024,1536]{1,0:T(8,128)(2,1)} %param.11) | copy-start | bytes 9437188
  1061.8 4.9 copy-start.1
Sparse Core Ops, SparseCore 0:
  40.3 55.2 all-reduce.1
where the time goes:
time: 1080 us; the launch traced here: 1070 us
  waiting for transfers between devices  400 us (37%)
  matrix products  315 us (29%)
  other arithmetic  152 us (14%)
  local copies, waits for them, and re-layouts  119 us (11%)
  blocking collectives  51.5 us (5%)
  starting transfers between devices  21.6 us (2%)
  between operations  14.4 us (1%)
    dot_general x16, matrix products, attend(): jnp.einsum('qd,kd->qk', queries, keys_part, preferred_element_type=jnp.fl...  156 us
    dot_general x16, matrix products, attend(): jnp.einsum('qk,kd->qd', weights, values_part, preferred_element_type=jnp....  141 us
    reduce_sum x16, other arithmetic, attend(): row_total = jnp.sum(raised, axis=1, keepdims=True)  130 us
    all_to_all x1, waiting for transfers between devices, body(): lax.all_to_all(spread(projected), 'tile', split_axis=0, concat_axis=2, ti...  95.2 us
    all_to_all x1, waiting for transfers between devices, body(): lax.all_to_all(spread(earlier), 'tile', split_axis=0, concat_axis=2, tile...  87.8 us
    all_to_all x1, waiting for transfers between devices, body(): lax.all_to_all(spread(following), 'tile', split_axis=0, concat_axis=2, ti...  85.3 us
    psum x1, waiting for transfers between devices, spread_2(): return lax.psum(jnp.where(mine, array, jnp.zeros_like(array)), axis)  55.4 us
    all_to_all x1, blocking collectives, body(): lax.all_to_all(outgoing, 'tile', split_axis=0, concat_axis=1, tiled=True)  51.5 us
  transfers between devices with their start and end apart: 7, of which 7 were waited for; matrix products, arithmetic and copies ran while one was open for 7% of the time, Pallas kernels for 0%

commit v1 on v0

v1 whole, which is shorter than its diff:
```python
import functools
import math

import jax
import jax.numpy as jnp
from jax import lax
from jax.experimental import pallas as pl
from jax.experimental.pallas import tpu as pltpu
from jax.sharding import PartitionSpec as P

HEADS = 8
HD = 128
BLK = 128
LOG_SCALE = math.log2(math.e) / math.sqrt(HD)
NT = (((1,), (1,)), ((), ()))


def attention_kernel(rows, chunk, epi_ref, q_ref, own_ref, earlier_ref, following_ref, anchor_ref,
                     out_ref, keys, values):
    tokens = own_ref.shape[0]
    slots = epi_ref.shape[1]
    step = pl.program_id(0)

    @pl.when(step == 0)
    def _():
        for part, (ref, first) in enumerate(
            ((own_ref, HD), (anchor_ref, 0), (earlier_ref, 0), (following_ref, 0))
        ):
            span = pl.ds(part * tokens, tokens)
            keys[span, :] = ref[:, first:first + HD]
            values[span, :HD] = ref[:, first + HD:first + 2 * HD]
            values[span, HD:] = jnp.ones((tokens, HD), values.dtype)

    queries = q_ref[:, :HD]

    def scores_of(query_rows, key_rows):
        return lax.dot_general(query_rows, key_rows, NT, preferred_element_type=jnp.float32)

    def fold(state, scores, value_rows):
        peak = jnp.max(scores, axis=1, keepdims=True) * LOG_SCALE
        if state is not None:
            peak = jnp.maximum(state[0], peak)
        weights = jnp.exp2(scores * LOG_SCALE - peak).astype(jnp.bfloat16)
        summed = jnp.dot(weights, value_rows, preferred_element_type=jnp.float32)
        if state is not None:
            summed = summed + state[1] * jnp.exp2(state[0] - peak)
        return peak, summed

    state = None
    for start in range(0, 2 * tokens, chunk):
        state = fold(state, scores_of(queries, keys[start:start + chunk, :]),
                     values[start:start + chunk, :])

    per_step = rows // BLK
    for sub in range(per_step):
        block = step * per_step + sub
        span = slice(sub * BLK, (sub + 1) * BLK)
        key_rows, value_rows, used = [], [], []
        for slot in range(slots):
            entry = epi_ref[block, slot]
            place = pl.multiple_of(2 * tokens + jnp.maximum(entry, 0) * BLK, BLK)
            key_rows.append(keys[pl.ds(place, BLK), :])
            value_rows.append(values[pl.ds(place, BLK), :])
            used.append(entry >= 0)
        scores = scores_of(queries[span], jnp.concatenate(key_rows, axis=0))
        scores = jnp.concatenate(
            [
                jnp.where(used[slot], scores[:, slot * BLK:(slot + 1) * BLK], -jnp.inf)
                for slot in range(slots)
            ],
            axis=1,
        )
        _, summed = fold((state[0][span], state[1][span]), scores,
                         jnp.concatenate(value_rows, axis=0))
        out_ref[span, :] = (summed[:, :HD] / summed[:, HD:]).astype(out_ref.dtype)


def attend(epi_rows, queries, own, earlier, following, anchored, rows=512, chunk=1024):
    tokens = own.shape[0]
    count = queries.shape[0]
    rows = min(rows, count)
    chunk = min(chunk, tokens)
    whole = lambda array: pl.BlockSpec(array.shape, lambda i: (0, 0))
    return pl.pallas_call(
        functools.partial(attention_kernel, rows, chunk),
        grid=(count // rows,),
        in_specs=[
            pl.BlockSpec(memory_space=pltpu.SMEM),
            pl.BlockSpec((rows, queries.shape[1]), lambda i: (i, 0)),
            whole(own), whole(earlier), whole(following), whole(anchored),
        ],
        out_specs=pl.BlockSpec((rows, HD), lambda i: (i, 0)),
        out_shape=jax.ShapeDtypeStruct((count, HD), jnp.bfloat16),
        scratch_shapes=[
            pltpu.VMEM((4 * tokens, HD), jnp.bfloat16),
            pltpu.VMEM((4 * tokens, 2 * HD), jnp.bfloat16),
        ],
        compiler_params=pltpu.CompilerParams(vmem_limit_bytes=48 * 1024 * 1024),
        cost_estimate=pl.CostEstimate(
            flops=4 * count * 3 * tokens * HD * 2,
            bytes_accessed=2 * HD * (9 * tokens + 2 * count),
            transcendentals=count * 3 * tokens,
        ),
    )(epi_rows, queries, own, earlier, following, anchored)


def spread_2(array, axis, root):
    mine = lax.axis_index(axis) == root
    return lax.psum(jnp.where(mine, array, jnp.zeros_like(array)), axis)


def from_behind(array, axis, by):
    count = lax.axis_size(axis)
    return lax.ppermute(array, axis, [(i, (i + by) % count) for i in range(count)])


def body(latents, qkv_weight, out_weight, anchor, epi_list):
    per_dev, tile_tokens, model_width = latents.shape
    tile_count = lax.axis_size("tile")
    view_tokens = tile_tokens * tile_count
    parts = tile_count // HEADS
    part_rows = view_tokens // parts
    shaped = qkv_weight.reshape(model_width, HEADS, 3 * HD)
    tile_index = lax.axis_index("tile")

    resident = []
    for view in range(per_dev):
        projected = jnp.einsum(
            "td,dhc->htc", latents[view], shaped, preferred_element_type=jnp.float32
        ).astype(jnp.bfloat16)
        wide = jnp.broadcast_to(projected[:, None], (HEADS, parts, tile_tokens, 3 * HD))
        received = lax.all_to_all(
            wide.reshape(tile_count, tile_tokens, 3 * HD), "tile",
            split_axis=0, concat_axis=0, tiled=True,
        )
        resident.append(received.reshape(view_tokens, 3 * HD))

    key_values = [array[:, HD:] for array in resident]
    target = anchor[0]
    anchored = key_values[0]
    for view in range(1, per_dev):
        anchored = jnp.where(target % per_dev == view, key_values[view], anchored)
    anchored = spread_2(anchored, "view", target // per_dev)
    before = from_behind(key_values[per_dev - 1], "view", 1)
    after = from_behind(key_values[0], "view", -1)
    around = [before] + key_values + [after]

    own_part = tile_index % parts
    outs = []
    for view in range(per_dev):
        queries = resident[view]
        if parts > 1:
            queries = lax.dynamic_slice_in_dim(queries, own_part * part_rows, part_rows, 0)
        epi_rows = epi_list[view]
        if parts > 1:
            blocks = part_rows // BLK
            epi_rows = lax.dynamic_slice_in_dim(epi_rows, own_part * blocks, blocks, 0)
        attended = attend(epi_rows, queries, resident[view], around[view], around[view + 2],
                          anchored)
        outgoing = attended.reshape(1, tile_count // parts, tile_tokens, HD)
        if parts > 1:
            mine = jnp.arange(parts, dtype=jnp.int32)[:, None, None, None] == own_part
            outgoing = jnp.where(mine, outgoing, jnp.zeros((), jnp.bfloat16))
        returned = lax.all_to_all(
            outgoing.reshape(tile_count, tile_tokens, HD), "tile",
            split_axis=0, concat_axis=0, tiled=True,
        ).reshape(HEADS, parts, tile_tokens, HD)
        home = tile_index // (tile_count // parts)
        returned = lax.dynamic_index_in_dim(returned, home, 1, keepdims=False)
        outs.append(
            jnp.einsum(
                "htc,hcd->td", returned, out_weight.reshape(HEADS, HD, model_width),
                preferred_element_type=jnp.float32,
            ).astype(jnp.bfloat16)
        )
    return jnp.stack(outs)


def solution(mesh):
    return jax.shard_map(
        body,
        mesh=mesh,
        in_specs=(P("view", "tile", None), P(), P(), P(), P("view", None, None)),
        out_specs=P("view", "tile", None),
        check_vma=False,
    )
```

time: 1080 us -> 403 us (0.37)
  matrix products: 315 us -> 41.4 us
  waiting for transfers between devices: 400 us -> 189 us
  other arithmetic: 152 us -> 6.53 us
  local copies, waits for them, and re-layouts: 119 us -> 43.3 us
  Pallas kernels: 0 us -> 64.9 us
  blocking collectives: 51.5 us -> 0 us
  starting transfers between devices: 21.6 us -> 41.7 us
    dot_general x34 -> x8, matrix products: 315 us -> 41.4 us  [the longest x4 30.5 us: body(): jnp.einsum('td,dhc->htc', latents[view], shaped, preferred_element_type=j...]
    all_to_all x4 -> x8, waiting for transfers between devices: 302 us -> 127 us  [the longest x4 120 us: body(): lax.all_to_all(wide.reshape(tile_count, tile_tokens, 3 * HD), 'tile', spl...]
    reduce_sum x16 -> x0, other arithmetic: 130 us -> none  [attend(): row_total = jnp.sum(raised, axis=1, keepdims=True)]
    pallas_call x0 -> x4, Pallas kernels: none -> 64.9 us  [attend(): pl.pallas_call(functools.partial(attention_kernel, rows, chunk), grid=(co...]
    all_to_all x1 -> x0, blocking collectives: 51.5 us -> none  [body(): lax.all_to_all(outgoing, 'tile', split_axis=0, concat_axis=1, tiled=True)]
    psum x1, waiting for transfers between devices: 55.4 us -> 29.8 us  [spread_2(): return lax.psum(jnp.where(mine, array, jnp.zeros_like(array)), axis)]
    all_to_all x4 -> x8, starting transfers between devices: 18.7 us -> 38.6 us  [the longest x4 19.3 us: body(): lax.all_to_all(outgoing.reshape(tile_count, tile_tokens, HD), 'tile', spl...]
    concatenate x3 -> x0, other arithmetic: 19.5 us -> none  [the longest x1 9.06 us: allowed_tokens(): return jnp.concatenate([always, nearby, always], axis=1)]
  transfers between devices with their start and end apart: 7 -> 11, of which waited for: 7 -> 7; matrix products, arithmetic and copies ran while one was open for 7% -> 10% of each run, Pallas kernels for 0% -> 16%
where the time goes in v1:
time: 403 us; the launch traced here: 401 us
  waiting for transfers between devices  189 us (47%)
  Pallas kernels  64.9 us (16%)
  local copies, waits for them, and re-layouts  43.3 us (11%)
  starting transfers between devices  41.7 us (10%)
  matrix products  41.4 us (10%)
  between operations  14.3 us (4%)
  other arithmetic  6.53 us (2%)
    all_to_all x4, waiting for transfers between devices, body(): lax.all_to_all(wide.reshape(tile_count, tile_tokens, 3 * HD), 'tile', spl...  120 us
    pallas_call x4, Pallas kernels, attend(): pl.pallas_call(functools.partial(attention_kernel, rows, chunk), grid=(co...  64.9 us
    ppermute x2, waiting for transfers between devices, from_behind(): lax.ppermute(array, axis, [(i, (i + by) % count) for i in range(count)])  32.3 us
    dot_general x4, matrix products, body(): jnp.einsum('td,dhc->htc', latents[view], shaped, preferred_element_type=j...  30.5 us
    psum x1, waiting for transfers between devices, spread_2(): return lax.psum(jnp.where(mine, array, jnp.zeros_like(array)), axis)  29.8 us
    unnamed x44, local copies, waits for them, and re-layouts  19.8 us
    all_to_all x4, starting transfers between devices, body(): lax.all_to_all(outgoing.reshape(tile_count, tile_tokens, HD), 'tile', spl...  19.3 us
    all_to_all x4, starting transfers between devices, body(): lax.all_to_all(wide.reshape(tile_count, tile_tokens, 3 * HD), 'tile', spl...  19.3 us
  transfers between devices with their start and end apart: 11, of which 7 were waited for; matrix products, arithmetic and copies ran while one was open for 10% of the time, Pallas kernels for 16%

profile of v1, /device:TPU:0, one launch (start us, length us, event | category | flops | bytes accessed | tf_op | source)
XLA Modules:
  0.0 400.9 jit_solution(3743271113343757087)
XLA Ops:
  6.5 12.8 %copy.22 = bf16[1536,3072]{0,1:T(8,128)(2,1)} copy(bf16[1536,3072]{1,0:T(8,128)(2,1)} %param.6) | data formatting | bytes 18874368 | tf_op jit(solution)/shard_map/reshape | solution.py:123
  19.3 7.6 %fusion.10 = bf16[8,256,384]{1,2,0:T(8,128)(2,1)} fusion(bf16[1536,8,384]{0,2,1:T(8,128)(2,1)} %bitcast.115, bf16[4,256,1536]{2,1,0:T(8,128)(2,1)} %param.5), kind=kOutput, calls=%fused_computation.19 | convolution fusion | flops 2416705536 | bytes 11796480 | tf_op jit(solution)/shard_map/td,dhc->htc/dot_general | solution.py:128
  26.9 6.3 %all-to-all-start.2 = ((bf16[8,256,384]{1,2,0:T(8,128)(2,1)}), bf16[8,256,384]{1,2,0:T(8,128)(2,1)}, u32[]{:S(2)}, u32[]{:S(2)}) async-start(bf16[8,256,384]{1,2,0:T(8,128)(2,1)} %fusion.10), calls=%async_computation.2 | async-start | bytes 3145728 | tf_op jit(solution)/shard_map/all_to_all | solution.py:132
  33.2 7.6 %fusion.11 = bf16[8,256,384]{1,2,0:T(8,128)(2,1)} fusion(bf16[1536,8,384]{0,2,1:T(8,128)(2,1)} %bitcast.116, bf16[4,256,1536]{2,1,0:T(8,128)(2,1)} %param.5), kind=kOutput, calls=%fused_computation.20 | convolution fusion | flops 2416705536 | bytes 11796480 | tf_op jit(solution)/shard_map/td,dhc->htc/dot_general | solution.py:128
  40.9 30.3 %all-to-all-done.2 = bf16[8,256,384]{1,2,0:T(8,128)(2,1)} async-done(((bf16[8,256,384]{1,2,0:T(8,128)(2,1)}), bf16[8,256,384]{1,2,0:T(8,128)(2,1)}, u32[]{:S(2)}, u32[]{:S(2)}) %all-to-all-start.2) | async-done | bytes 1572896 | tf_op jit(solution)/shard_map/all_to_all | solution.py:132
  71.2 4.3 %all-to-all-start.3 = ((bf16[8,256,384]{1,2,0:T(8,128)(2,1)}), bf16[8,256,384]{1,2,0:T(8,128)(2,1)}, u32[]{:S(2)}, u32[]{:S(2)}) async-start(bf16[8,256,384]{1,2,0:T(8,128)(2,1)} %fusion.11), calls=%async_computation.3 | async-start | bytes 3145728 | tf_op jit(solution)/shard_map/all_to_all | solution.py:132
  75.5 7.6 %fusion.8 = bf16[8,256,384]{1,2,0:T(8,128)(2,1)} fusion(bf16[1536,8,384]{0,2,1:T(8,128)(2,1)} %bitcast.117, bf16[4,256,1536]{2,1,0:T(8,128)(2,1)} %param.5), kind=kOutput, calls=%fused_computation.17 | convolution fusion | flops 2416705536 | bytes 11796480 | tf_op jit(solution)/shard_map/td,dhc->htc/dot_general | solution.py:128
  83.1 30.2 %all-to-all-done.3 = bf16[8,256,384]{1,2,0:T(8,128)(2,1)} async-done(((bf16[8,256,384]{1,2,0:T(8,128)(2,1)}), bf16[8,256,384]{1,2,0:T(8,128)(2,1)}, u32[]{:S(2)}, u32[]{:S(2)}) %all-to-all-start.3) | async-done | bytes 1572896 | tf_op jit(solution)/shard_map/all_to_all | solution.py:132
  113.3 4.3 %all-to-all-start = ((bf16[8,256,384]{1,2,0:T(8,128)(2,1)}), bf16[8,256,384]{1,2,0:T(8,128)(2,1)}, u32[]{:S(2)}, u32[]{:S(2)}) async-start(bf16[8,256,384]{1,2,0:T(8,128)(2,1)} %fusion.8), calls=%async_computation | async-start | bytes 3145728 | tf_op jit(solution)/shard_map/all_to_all | solution.py:132
  117.6 7.6 %fusion.9 = bf16[8,256,384]{1,2,0:T(8,128)(2,1)} fusion(bf16[1536,8,384]{0,2,1:T(8,128)(2,1)} %bitcast.118, bf16[4,256,1536]{2,1,0:T(8,128)(2,1)} %param.5), kind=kOutput, calls=%fused_computation.18 | convolution fusion | flops 2416705536 | bytes 11796480 | tf_op jit(solution)/shard_map/td,dhc->htc/dot_general | solution.py:128
  125.2 30.2 %all-to-all-done = bf16[8,256,384]{1,2,0:T(8,128)(2,1)} async-done(((bf16[8,256,384]{1,2,0:T(8,128)(2,1)}), bf16[8,256,384]{1,2,0:T(8,128)(2,1)}, u32[]{:S(2)}, u32[]{:S(2)}) %all-to-all-start) | async-done | bytes 1572896 | tf_op jit(solution)/shard_map/all_to_all | solution.py:132
  155.5 4.3 %all-to-all-start.1 = ((bf16[8,256,384]{1,2,0:T(8,128)(2,1)}), bf16[8,256,384]{1,2,0:T(8,128)(2,1)}, u32[]{:S(2)}, u32[]{:S(2)}) async-start(bf16[8,256,384]{1,2,0:T(8,128)(2,1)} %fusion.9), calls=%async_computation.1 | async-start | bytes 3145728 | tf_op jit(solution)/shard_map/all_to_all | solution.py:132
  160.5 2.6 copy.12
  163.1 2.6 copy.14
  165.7 2.6 copy.8
  168.3 29.3 %all-to-all-done.1 = bf16[8,256,384]{1,2,0:T(8,128)(2,1)} async-done(((bf16[8,256,384]{1,2,0:T(8,128)(2,1)}), bf16[8,256,384]{1,2,0:T(8,128)(2,1)}, u32[]{:S(2)}, u32[]{:S(2)}) %all-to-all-start.1) | async-done | bytes 1572896 | tf_op jit(solution)/shard_map/all_to_all | solution.py:132
  197.6 2.6 copy.10
  200.2 4.6 %fusion.20 = (bf16[2048,256]{1,0:T(8,128)(2,1)}, bf16[2048,256]{1,0:T(8,128)(2,1)}, bf16[2048,256]{1,0:T(8,128)(2,1)}, bf16[2048,256]{1,0:T(8,128)(2,1)}, bf16[2048,256]{1,0:T(8,128)(2,1)}) fusion(bf16[2048,384]{1,0:T(8,128)(2,1)} %bitcast.95, bf16[2048,384]{1,0:T(8,128)(2,1)} %bitcast.104, bf16[2048,384]{1,0:T(8,128)(2,1)} %bitcast.101, pred[]{:T(512)S(6)} %eq.19, ...), kind=kLoop, calls=%fused_computation.30 | loop fusion | flops 2097152 | bytes 9437188 | tf_op jit(solution)/shard_map/slice | solution.py:138
  204.8 1.5 collective-permute-start
  206.7 1.6 collective-permute-start.1
  208.3 32.3 %collective-permute-done.earlier_ref = bf16[2048,256]{1,0:T(8,128)(2,1)} collective-permute-done((bf16[2048,256]{1,0:T(8,128)(2,1)}, bf16[2048,256]{1,0:T(8,128)(2,1)}, u32[]{:S(2)}, u32[]{:S(2)}) %collective-permute-start) | collective-permute-done | bytes 1048608 | tf_op jit(solution)/shard_map/ppermute | solution.py:114
  240.6 29.8 %all-reduce.2.cloned.1.call-done.anchor_ref = bf16[2048,256]{1,0:T(8,128)(2,1)} async-done(((bf16[2048,256]{1,0:T(8,128)(2,1)}), bf16[2048,256]{1,0:T(8,128)(2,1)}) %all-reduce.2.cloned.1.call-update) | async-done | bytes 1048592 | tf_op jit(solution)/shard_map/psum | solution.py:109
  270.4 1.4 copy-done.4
  271.8 1.2 copy-done.8
  273.0 1.2 copy-done.14
  274.2 16.4 %shard_map.55 = bf16[2048,128]{1,0:T(8,128)(2,1)S(1)} custom-call(s32[16,6]{1,0:T(8,128)S(1)} %bitcast.114, bf16[2048,384]{1,0:T(8,128)(2,1)S(1)} %bitcast.105, bf16[2048,384]{1,0:T(8,128)(2,1)S(1)} %bitcast.106, bf16[2048,256]{1,0:T(8,128)(2,1)} %collective-permute-done.earlier_ref, bf16[2048,256]{1,0:T(8,128)(2,1)S(1)} %copy-done.8, ...), custom_call_target="tpu_custom_call" | custom-call | flops 12884901888 | bytes 5767168 | tf_op jit(solution)/shard_map/pallas_call | solution.py:84
  291.4 4.1 %all-to-all-start.4 = ((bf16[8,256,128]{2,1,0:T(8,128)(2,1)}), bf16[8,256,128]{2,1,0:T(8,128)(2,1)}, u32[]{:S(2)}, u32[]{:S(2)}) async-start(bf16[8,256,128]{2,1,0:T(8,128)(2,1)} %bitcast.110), calls=%async_computation.4 | async-start | bytes 1048576 | tf_op jit(solution)/shard_map/all_to_all | solution.py:164
  295.6 1.4 copy-done.3
  297.0 1.2 copy-done.5
  298.2 1.2 copy-done.7
  299.4 1.2 copy-done.15
  300.6 15.8 %shard_map.56 = bf16[2048,128]{1,0:T(8,128)(2,1)S(1)} custom-call(s32[16,6]{1,0:T(8,128)S(1)} %bitcast.113, bf16[2048,384]{1,0:T(8,128)(2,1)S(1)} %bitcast.102, bf16[2048,384]{1,0:T(8,128)(2,1)S(1)} %bitcast.103, bf16[2048,256]{1,0:T(8,128)(2,1)S(1)} %copy-done.7, bf16[2048,256]{1,0:T(8,128)(2,1)S(1)} %copy-done.5, bf16[2048,256]{1,0:T(8,128)(2,1)S(1)} %copy-done.15), custom_call_target="tpu_custom_call" | custom-call | flops 12884901888 | bytes 5767168 | tf_op jit(solution)/shard_map/pallas_call | solution.py:84
  317.2 5.0 %all-to-all-start.5 = ((bf16[8,256,128]{2,1,0:T(8,128)(2,1)}), bf16[8,256,128]{2,1,0:T(8,128)(2,1)}, u32[]{:S(2)}, u32[]{:S(2)}) async-start(bf16[8,256,128]{2,1,0:T(8,128)(2,1)} %bitcast.109), calls=%async_computation.5 | async-start | bytes 1048576 | tf_op jit(solution)/shard_map/all_to_all | solution.py:164
  322.2 1.4 copy-done.2
  323.7 1.2 copy-done.9
  324.9 1.2 copy-done.16
  326.1 16.4 %shard_map.57 = bf16[2048,128]{1,0:T(8,128)(2,1)S(1)} custom-call(s32[16,6]{1,0:T(8,128)S(1)} %bitcast.112, bf16[2048,384]{1,0:T(8,128)(2,1)S(1)} %bitcast.99, bf16[2048,384]{1,0:T(8,128)(2,1)S(1)} %bitcast.100, bf16[2048,256]{1,0:T(8,128)(2,1)S(1)} %copy-done.9, bf16[2048,256]{1,0:T(8,128)(2,1)} %get-tuple-element.5.following_ref, ...), custom_call_target="tpu_custom_call" | custom-call | flops 12884901888 | bytes 5767168 | tf_op jit(solution)/shard_map/pallas_call | solution.py:84
  343.3 5.1 %all-to-all-start.6 = ((bf16[8,256,128]{2,1,0:T(8,128)(2,1)}), bf16[8,256,128]{2,1,0:T(8,128)(2,1)}, u32[]{:S(2)}, u32[]{:S(2)}) async-start(bf16[8,256,128]{2,1,0:T(8,128)(2,1)} %bitcast.107), calls=%async_computation.6 | async-start | bytes 1048576 | tf_op jit(solution)/shard_map/all_to_all | solution.py:164
  348.4 1.4 copy-done.1
  349.8 1.2 copy-done.6
  352.2 16.4 %shard_map.58 = bf16[2048,128]{1,0:T(8,128)(2,1)S(1)} custom-call(s32[16,6]{1,0:T(8,128)S(1)} %bitcast.111, bf16[2048,384]{1,0:T(8,128)(2,1)S(1)} %bitcast.96, bf16[2048,384]{1,0:T(8,128)(2,1)S(1)} %bitcast.97, bf16[2048,256]{1,0:T(8,128)(2,1)S(1)} %copy-done.6, bf16[2048,256]{1,0:T(8,128)(2,1)} %collective-permute-done.1.following_ref, ...), custom_call_target="tpu_custom_call" | custom-call | flops 12884901888 | bytes 5767168 | tf_op jit(solution)/shard_map/pallas_call | solution.py:84
  369.4 5.1 %all-to-all-start.7 = ((bf16[8,256,128]{2,1,0:T(8,128)(2,1)}), bf16[8,256,128]{2,1,0:T(8,128)(2,1)}, u32[]{:S(2)}, u32[]{:S(2)}) async-start(bf16[8,256,128]{2,1,0:T(8,128)(2,1)} %bitcast.108), calls=%async_computation.7 | async-start | bytes 1048576 | tf_op jit(solution)/shard_map/all_to_all | solution.py:164
  374.5 2.9 fusion.7
  377.4 2.9 fusion.6
  380.4 2.9 fusion.5
  383.3 6.7 %all-to-all-done.7 = bf16[8,256,128]{2,1,0:T(8,128)(2,1)} async-done(((bf16[8,256,128]{2,1,0:T(8,128)(2,1)}), bf16[8,256,128]{2,1,0:T(8,128)(2,1)}, u32[]{:S(2)}, u32[]{:S(2)}) %all-to-all-start.7) | async-done | bytes 524320 | tf_op jit(solution)/shard_map/all_to_all | solution.py:164
  390.0 2.2 fusion.4
  392.2 1.9 pad_maximum_fusion
  (43 shorter events, 4.9 us)
Async XLA Ops:
  6.5 368.0 %copy-start = (bf16[1024,1536]{1,0:T(8,128)(2,1)S(1)}, bf16[1024,1536]{1,0:T(8,128)(2,1)}, u32[]{:S(2)}) copy-start(bf16[1024,1536]{1,0:T(8,128)(2,1)} %param.7) | copy-start | bytes 9437188
  26.9 44.3 %all-to-all-start.2 = ((bf16[8,256,384]{1,2,0:T(8,128)(2,1)}), bf16[8,256,384]{1,2,0:T(8,128)(2,1)}, u32[]{:S(2)}, u32[]{:S(2)}) async-start(bf16[8,256,384]{1,2,0:T(8,128)(2,1)} %fusion.10), calls=%async_computation.2 | async-start | bytes 3145728 | tf_op jit(solution)/shard_map/all_to_all | solution.py:132
  71.2 42.1 %all-to-all-start.3 = ((bf16[8,256,384]{1,2,0:T(8,128)(2,1)}), bf16[8,256,384]{1,2,0:T(8,128)(2,1)}, u32[]{:S(2)}, u32[]{:S(2)}) async-start(bf16[8,256,384]{1,2,0:T(8,128)(2,1)} %fusion.11), calls=%async_computation.3 | async-start | bytes 3145728 | tf_op jit(solution)/shard_map/all_to_all | solution.py:132
  113.3 42.2 %all-to-all-start = ((bf16[8,256,384]{1,2,0:T(8,128)(2,1)}), bf16[8,256,384]{1,2,0:T(8,128)(2,1)}, u32[]{:S(2)}, u32[]{:S(2)}) async-start(bf16[8,256,384]{1,2,0:T(8,128)(2,1)} %fusion.8), calls=%async_computation | async-start | bytes 3145728 | tf_op jit(solution)/shard_map/all_to_all | solution.py:132
  155.5 42.1 %all-to-all-start.1 = ((bf16[8,256,384]{1,2,0:T(8,128)(2,1)}), bf16[8,256,384]{1,2,0:T(8,128)(2,1)}, u32[]{:S(2)}, u32[]{:S(2)}) async-start(bf16[8,256,384]{1,2,0:T(8,128)(2,1)} %fusion.9), calls=%async_computation.1 | async-start | bytes 3145728 | tf_op jit(solution)/shard_map/all_to_all | solution.py:132
  159.8 110.6 %all-reduce.2.cloned.1.call-start = ((), (), s32[]{:S(2)}) async-start(), calls=%async_computation.8 | async-start | bytes 2097152 | tf_op jit(solution)/shard_map/psum | solution.py:109
  200.2 6.2 %copy-start.21 = (s32[4,16,6]{1,0,2:T(4,128)S(1)}, s32[4,16,6]{1,0,2:T(4,128)}, u32[]{:S(2)}) copy-start(s32[4,16,6]{1,0,2:T(4,128)} %param.9) | copy-start | bytes 4612
  204.8 35.7 %collective-permute-start = (bf16[2048,256]{1,0:T(8,128)(2,1)}, bf16[2048,256]{1,0:T(8,128)(2,1)}, u32[]{:S(2)}, u32[]{:S(2)}) collective-permute-start(bf16[2048,256]{1,0:T(8,128)(2,1)} %get-tuple-element.5.following_ref), channel_id=1, source_target_pairs={{0,8},{8,16},{16,24},{24,0},{1,9},{9,17},{17,25},{25,1},{2,10},{10... | collective-permute-start | bytes 3145736 | tf_op jit(solution)/shard_map/ppermute | solution.py:114
  206.7 141.7 %collective-permute-start.1 = (bf16[2048,256]{1,0:T(8,128)(2,1)}, bf16[2048,256]{1,0:T(8,128)(2,1)}, u32[]{:S(2)}, u32[]{:S(2)}) collective-permute-start(bf16[2048,256]{1,0:T(8,128)(2,1)} %get-tuple-element.9.earlier_ref), channel_id=1, source_target_pairs={{0,24},{8,0},{16,8},{24,16},{1,25},{9,1},{17,9},{25,17},{2,26},{10... | collective-permute-start | bytes 3145736 | tf_op jit(solution)/shard_map/ppermute | solution.py:114
  270.4 1.4 copy-start.4
  271.8 1.2 copy-start.8
  273.0 1.2 copy-start.14
  290.6 0.8 copy-start.13
  291.4 25.8 %all-to-all-start.4 = ((bf16[8,256,128]{2,1,0:T(8,128)(2,1)}), bf16[8,256,128]{2,1,0:T(8,128)(2,1)}, u32[]{:S(2)}, u32[]{:S(2)}) async-start(bf16[8,256,128]{2,1,0:T(8,128)(2,1)} %bitcast.110), calls=%async_computation.4 | async-start | bytes 1048576 | tf_op jit(solution)/shard_map/all_to_all | solution.py:164
  295.5 1.4 copy-start.3
  297.0 1.2 copy-start.5
  298.2 1.2 copy-start.7
  299.4 1.2 copy-start.15
  316.4 0.8 copy-start.12
  317.2 26.0 %all-to-all-start.5 = ((bf16[8,256,128]{2,1,0:T(8,128)(2,1)}), bf16[8,256,128]{2,1,0:T(8,128)(2,1)}, u32[]{:S(2)}, u32[]{:S(2)}) async-start(bf16[8,256,128]{2,1,0:T(8,128)(2,1)} %bitcast.109), calls=%async_computation.5 | async-start | bytes 1048576 | tf_op jit(solution)/shard_map/all_to_all | solution.py:164
  322.2 1.4 copy-start.2
  323.7 1.2 copy-start.9
  324.9 1.2 copy-start.16
  342.5 0.8 copy-start.10
  343.3 26.1 %all-to-all-start.6 = ((bf16[8,256,128]{2,1,0:T(8,128)(2,1)}), bf16[8,256,128]{2,1,0:T(8,128)(2,1)}, u32[]{:S(2)}, u32[]{:S(2)}) async-start(bf16[8,256,128]{2,1,0:T(8,128)(2,1)} %bitcast.107), calls=%async_computation.6 | async-start | bytes 1048576 | tf_op jit(solution)/shard_map/all_to_all | solution.py:164
  348.4 1.4 copy-start.1
  349.8 1.2 copy-start.6
  351.0 1.2 copy-start.17
  368.6 0.8 copy-start.11
  369.4 20.6 %all-to-all-start.7 = ((bf16[8,256,128]{2,1,0:T(8,128)(2,1)}), bf16[8,256,128]{2,1,0:T(8,128)(2,1)}, u32[]{:S(2)}, u32[]{:S(2)}) async-start(bf16[8,256,128]{2,1,0:T(8,128)(2,1)} %bitcast.108), calls=%async_computation.7 | async-start | bytes 1048576 | tf_op jit(solution)/shard_map/all_to_all | solution.py:164
  390.0 2.2 copy-start.18
  390.0 2.2 copy-start.19
  390.0 2.2 copy-start.20
Sparse Core Ops, SparseCore 0:
  206.5 63.8 all-reduce.1

commit v2 on v0

v2 whole, which is shorter than its diff:
```python
import functools
import math

import jax
import jax.numpy as jnp
import numpy as np
from jax import lax
from jax.experimental import pallas as pl
from jax.experimental.pallas import tpu as pltpu
from jax.sharding import PartitionSpec as P

HEADS = 8
HD = 128
BLK = 128
LOG_SCALE = math.log2(math.e) / math.sqrt(HD)
NT = (((1,), (1,)), ((), ()))


def spread_2(array, axis, root):
    mine = lax.axis_index(axis) == root
    return lax.psum(jnp.where(mine, array, jnp.zeros_like(array)), axis)


def from_behind(array, axis, by):
    count = lax.axis_size(axis)
    return lax.ppermute(array, axis, [(i, (i + by) % count) for i in range(count)])


def project_kernel(view_ref, tokens_ref, weight_ref, out_ref):
    out_ref[0] = jnp.dot(
        tokens_ref[0], weight_ref[...], preferred_element_type=jnp.float32
    ).astype(out_ref.dtype)


def project(view, latents, weight):
    _, tokens, width = latents.shape
    return pl.pallas_call(
        project_kernel,
        grid_spec=pltpu.PrefetchScalarGridSpec(
            num_scalar_prefetch=1,
            grid=(HEADS,),
            in_specs=[
                pl.BlockSpec((1, tokens, width), lambda h, view: (view[0], 0, 0)),
                pl.BlockSpec((width, 3 * HD), lambda h, view: (0, h)),
            ],
            out_specs=pl.BlockSpec((1, tokens, 3 * HD), lambda h, view: (h, 0, 0)),
        ),
        out_shape=jax.ShapeDtypeStruct((HEADS, tokens, 3 * HD), jnp.bfloat16),
        compiler_params=pltpu.CompilerParams(vmem_limit_bytes=24 * 1024 * 1024),
        cost_estimate=pl.CostEstimate(
            flops=2 * tokens * width * HEADS * 3 * HD,
            bytes_accessed=2 * HEADS * 3 * HD * (width + tokens),
            transcendentals=0,
        ),
    )(view.reshape(1), latents, weight)


def scores_of(query_rows, key_rows):
    return lax.dot_general(query_rows, key_rows, NT, preferred_element_type=jnp.float32)


def fold(state, scores, value_rows):
    peak = jnp.max(scores, axis=1, keepdims=True) * LOG_SCALE
    if state is not None:
        peak = jnp.maximum(state[0], peak)
    weights = jnp.exp2(scores * LOG_SCALE - peak).astype(jnp.bfloat16)
    summed = jnp.dot(weights, value_rows, preferred_element_type=jnp.float32)
    if state is not None:
        summed = summed + state[1] * jnp.exp2(state[0] - peak)
    return peak, summed


def dense_kernel(chunk, q_ref, own_k, own_v, anchor_k, anchor_v, sum_ref, stat_ref, values):
    tokens = own_k.shape[0]

    @pl.when(pl.program_id(0) == 0)
    def _():
        values[:tokens, :HD] = own_v[...]
        values[tokens:, :HD] = anchor_v[...]
        values[:, HD:] = jnp.ones((2 * tokens, HD), values.dtype)

    queries = q_ref[...]
    state = None
    for part, key_ref in enumerate((own_k, anchor_k)):
        for start in range(0, tokens, chunk):
            first = part * tokens + start
            state = fold(state, scores_of(queries, key_ref[start:start + chunk, :]),
                         values[first:first + chunk, :])
    peak, summed = state
    sum_ref[...] = summed[:, :HD]
    lane = lax.broadcasted_iota(jnp.int32, stat_ref.shape, 1)
    stat_ref[...] = jnp.where(lane < HD // 2, summed[:, HD:], peak)


def dense(queries, own, anchored, rows=512, chunk=1024):
    tokens = own.shape[0]
    count = queries.shape[0]
    rows = min(rows, count)
    chunk = min(chunk, tokens)
    column = lambda c: pl.BlockSpec((tokens, HD), lambda i: (0, c))
    by_rows = pl.BlockSpec((rows, HD), lambda i: (i, 0))
    return pl.pallas_call(
        functools.partial(dense_kernel, chunk),
        grid=(count // rows,),
        in_specs=[by_rows, column(1), column(2), column(0), column(1)],
        out_specs=[by_rows, by_rows],
        out_shape=[jax.ShapeDtypeStruct((count, HD), jnp.float32)] * 2,
        scratch_shapes=[pltpu.VMEM((2 * tokens, 2 * HD), jnp.bfloat16)],
        compiler_params=pltpu.CompilerParams(vmem_limit_bytes=40 * 1024 * 1024),
        cost_estimate=pl.CostEstimate(
            flops=8 * count * 2 * tokens * HD,
            bytes_accessed=8 * HD * tokens + 10 * HD * count,
            transcendentals=count * 2 * tokens,
        ),
    )(queries, own, own, anchored, anchored)


def nearby_kernel(local, pick_ref, epi_ref, q_ref, sum_ref, stat_ref, *refs):
    sources, (out_ref, near, sems) = refs[:-3], refs[-3:]
    tokens = near.shape[0] // 2
    rows = q_ref.shape[0]
    slots = epi_ref.shape[1]
    step = pl.program_id(0)

    @pl.when(step == 0)
    def _():
        for side in range(2):
            for index, source in enumerate(sources):
                first = HD if index < local else 0

                @pl.when(pick_ref[side] == index)
                def _():
                    pltpu.make_async_copy(
                        source.at[:, pl.ds(first, 2 * HD)],
                        near.at[pl.ds(side * tokens, tokens), :], sems.at[side],
                    ).start()
        for side in range(2):
            pltpu.make_async_copy(
                sources[-1], near.at[pl.ds(side * tokens, tokens), :], sems.at[side]
            ).wait()

    per_step = rows // BLK
    ones = jnp.ones((BLK, HD), near.dtype)
    for sub in range(per_step):
        block = step * per_step + sub
        span = slice(sub * BLK, (sub + 1) * BLK)
        key_rows, value_rows, used = [], [], []
        for slot in range(slots):
            entry = epi_ref[block, slot]
            place = pl.multiple_of(jnp.maximum(entry, 0) * BLK, BLK)
            key_rows.append(near[pl.ds(place, BLK), :HD])
            value_rows.append(
                jnp.concatenate([near[pl.ds(place, BLK), HD:], ones], axis=1)
            )
            used.append(entry >= 0)
        scores = scores_of(q_ref[span, :], jnp.concatenate(key_rows, axis=0))
        scores = jnp.concatenate(
            [
                jnp.where(used[slot], scores[:, slot * BLK:(slot + 1) * BLK], -jnp.inf)
                for slot in range(slots)
            ],
            axis=1,
        )
        peak = stat_ref[span, HD // 2:HD // 2 + 1]
        total = jnp.broadcast_to(stat_ref[span, 0:1], (BLK, HD))
        state = (peak, jnp.concatenate([sum_ref[span, :], total], axis=1))
        _, summed = fold(state, scores, jnp.concatenate(value_rows, axis=0))
        out_ref[span, :] = (summed[:, :HD] / summed[:, HD:]).astype(out_ref.dtype)


def nearby(picks, epi_rows, queries, sums, stats, sources, rows=512):
    count = queries.shape[0]
    tokens = sources[0].shape[0]
    rows = min(rows, count)
    by_rows = pl.BlockSpec((rows, HD), lambda i: (i, 0))
    slots = epi_rows.shape[1]
    return pl.pallas_call(
        functools.partial(nearby_kernel, len(sources) - 2),
        grid=(count // rows,),
        in_specs=[pl.BlockSpec(memory_space=pltpu.SMEM)] * 2 + [by_rows] * 3
        + [pl.BlockSpec(memory_space=pl.ANY)] * len(sources),
        out_specs=by_rows,
        out_shape=jax.ShapeDtypeStruct((count, HD), jnp.bfloat16),
        scratch_shapes=[
            pltpu.VMEM((2 * tokens, 2 * HD), jnp.bfloat16),
            pltpu.SemaphoreType.DMA((2,)),
        ],
        compiler_params=pltpu.CompilerParams(vmem_limit_bytes=24 * 1024 * 1024),
        cost_estimate=pl.CostEstimate(
            flops=8 * count * slots * BLK * HD,
            bytes_accessed=8 * HD * tokens + 12 * HD * count,
            transcendentals=count * slots * BLK,
        ),
    )(picks, epi_rows, queries, sums, stats, *sources)


def order_table(count):
    table = []
    for first in range(count):
        order = [first]
        for view in [0, count - 1] + list(range(count)):
            if view not in order:
                order.append(view)
        table.append(order)
    return np.array(table, np.int32)


def body(latents, qkv_weight, out_weight, anchor, epi_list):
    per_dev, tile_tokens, model_width = latents.shape
    tile_count = lax.axis_size("tile")
    view_tokens = tile_tokens * tile_count
    parts = tile_count // HEADS
    part_rows = view_tokens // parts
    tile_index = lax.axis_index("tile")
    own_part = tile_index % parts
    target = anchor[0]

    table = order_table(per_dev)
    order = jnp.asarray(table)[target % per_dev]
    where_is = jnp.asarray(np.argsort(table, axis=1).astype(np.int32))[target % per_dev]

    def chosen(arrays, index):
        result = arrays[0]
        for place in range(1, len(arrays)):
            result = jnp.where(index == place, arrays[place], result)
        return result

    resident = []
    for slot in range(per_dev):
        projected = project(order[slot], latents, qkv_weight)
        wide = jnp.broadcast_to(projected[:, None], (HEADS, parts, tile_tokens, 3 * HD))
        wide = wide.reshape(tile_count, tile_tokens, 3 * HD)
        if resident:
            wide, resident[-1] = lax.optimization_barrier((wide, resident[-1]))
        received = lax.all_to_all(wide, "tile", split_axis=0, concat_axis=0, tiled=True)
        resident.append(received.reshape(view_tokens, 3 * HD))

    anchored = spread_2(resident[0][:, HD:], "view", target // per_dev)
    edge = min(3, per_dev)
    key_values = [array[:, HD:] for array in resident[:edge]]
    before = from_behind(chosen(key_values, where_is[per_dev - 1]), "view", 1)
    after = from_behind(chosen(key_values, where_is[0]), "view", -1)
    sources = resident + [before, after]

    out = jnp.zeros(latents.shape, jnp.bfloat16)
    home = tile_index // (tile_count // parts)
    for slot in range(per_dev):
        view = order[slot]
        queries = resident[slot]
        epi_rows = lax.dynamic_index_in_dim(epi_list, view, 0, keepdims=False)
        if parts > 1:
            blocks = part_rows // BLK
            queries = lax.dynamic_slice_in_dim(queries, own_part * part_rows, part_rows, 0)
            epi_rows = lax.dynamic_slice_in_dim(epi_rows, own_part * blocks, blocks, 0)
        sums, stats = dense(queries, resident[slot], anchored)
        earlier = jnp.where(view == 0, per_dev, where_is[jnp.maximum(view - 1, 0)])
        following = jnp.where(
            view == per_dev - 1, per_dev + 1, where_is[jnp.minimum(view + 1, per_dev - 1)]
        )
        picks = jnp.stack([earlier, following]).astype(jnp.int32)
        attended = nearby(picks, epi_rows, queries, sums, stats, sources)
        outgoing = attended.reshape(1, tile_count // parts, tile_tokens, HD)
        if parts > 1:
            mine = jnp.arange(parts, dtype=jnp.int32)[:, None, None, None] == own_part
            outgoing = jnp.where(mine, outgoing, jnp.zeros((), jnp.bfloat16))
        returned = lax.all_to_all(
            outgoing.reshape(tile_count, tile_tokens, HD), "tile",
            split_axis=0, concat_axis=0, tiled=True,
        ).reshape(HEADS, parts, tile_tokens, HD)
        returned = lax.dynamic_index_in_dim(returned, home, 1, keepdims=False)
        result = jnp.einsum(
            "htc,hcd->td", returned, out_weight.reshape(HEADS, HD, model_width),
            preferred_element_type=jnp.float32,
        ).astype(jnp.bfloat16)
        out = lax.dynamic_update_index_in_dim(out, result, view, 0)
    return out


def solution(mesh):
    return jax.shard_map(
        body,
        mesh=mesh,
        in_specs=(P("view", "tile", None), P(), P(), P(), P("view", None, None)),
        out_specs=P("view", "tile", None),
        check_vma=False,
    )
```

time: 1080 us -> 375 us (0.35)
  matrix products: 315 us -> 11.6 us
  waiting for transfers between devices: 400 us -> 120 us
  other arithmetic: 152 us -> 3.92 us
  Pallas kernels: 0 us -> 111 us
  local copies, waits for them, and re-layouts: 119 us -> 44.6 us
  blocking collectives: 51.5 us -> 0 us
  between operations: 14.4 us -> 39.9 us
  starting transfers between devices: 21.6 us -> 42.1 us
    dot_general x34 -> x4, matrix products: 315 us -> 11.6 us  [body(): jnp.einsum('htc,hcd->td', returned, out_weight.reshape(HEADS, HD, model_w...]
    all_to_all x4 -> x8, waiting for transfers between devices: 302 us -> 78.2 us  [the longest x4 73.3 us: body(): lax.all_to_all(wide, 'tile', split_axis=0, concat_axis=0, tiled=True)]
    reduce_sum x16 -> x0, other arithmetic: 130 us -> none  [attend(): row_total = jnp.sum(raised, axis=1, keepdims=True)]
    pallas_call x0 -> x12, Pallas kernels: none -> 111 us  [the longest x4 56.6 us: dense(): pl.pallas_call(functools.partial(dense_kernel, chunk), grid=(count // row...]
    all_to_all x1 -> x0, blocking collectives: 51.5 us -> none  [body(): lax.all_to_all(outgoing, 'tile', split_axis=0, concat_axis=1, tiled=True)]
    ppermute x2, waiting for transfers between devices: 42.5 us -> 0.01 us  [from_behind(): lax.ppermute(array, axis, [(i, (i + by) % count) for i in range(count)])]
    unnamed x16 -> x54, local copies, waits for them, and re-layouts: 11.7 us -> 39.5 us
    all_to_all x4 -> x8, starting transfers between devices: 18.7 us -> 39.1 us  [the longest x4 19.9 us: body(): lax.all_to_all(outgoing.reshape(tile_count, tile_tokens, HD), 'tile', spl...]
  transfers between devices with their start and end apart: 7 -> 11, of which waited for: 7 -> 5; matrix products, arithmetic and copies ran while one was open for 7% -> 4% of each run, Pallas kernels for 0% -> 26%
where the time goes in v2:
time: 375 us; the launch traced here: 373 us
  waiting for transfers between devices  120 us (32%)
  Pallas kernels  111 us (30%)
  local copies, waits for them, and re-layouts  44.6 us (12%)
  starting transfers between devices  42.1 us (11%)
  between operations  39.9 us (11%)
  matrix products  11.6 us (3%)
  other arithmetic  3.92 us (1%)
    all_to_all x4, waiting for transfers between devices, body(): lax.all_to_all(wide, 'tile', split_axis=0, concat_axis=0, tiled=True)  73.3 us
    pallas_call x4, Pallas kernels, dense(): pl.pallas_call(functools.partial(dense_kernel, chunk), grid=(count // row...  56.6 us
    psum x1, waiting for transfers between devices, spread_2(): return lax.psum(jnp.where(mine, array, jnp.zeros_like(array)), axis)  41.7 us
    unnamed x54, local copies, waits for them, and re-layouts  39.5 us
    pallas_call x4, Pallas kernels, nearby(): pl.pallas_call(functools.partial(nearby_kernel, len(sources) - 2), grid=(...  27.5 us
    pallas_call x4, Pallas kernels, project(): pl.pallas_call(project_kernel, grid_spec=pltpu.PrefetchScalarGridSpec(num...  26.6 us
    all_to_all x4, starting transfers between devices, body(): lax.all_to_all(outgoing.reshape(tile_count, tile_tokens, HD), 'tile', spl...  19.9 us
    all_to_all x4, starting transfers between devices, body(): lax.all_to_all(wide, 'tile', split_axis=0, concat_axis=0, tiled=True)  19.2 us
  transfers between devices with their start and end apart: 11, of which 5 were waited for; matrix products, arithmetic and copies ran while one was open for 4% of the time, Pallas kernels for 26%

profile of v2, /device:TPU:0, one launch (start us, length us, event | category | flops | bytes accessed | tf_op | source)
XLA Modules:
  0.0 372.8 jit_solution(1096803429844711489)
XLA Ops:
  8.9 3.7 copy-done.1
  12.5 1.9 copy-done.5
  14.4 6.7 %shard_map.74 = bf16[8,256,384]{2,1,0:T(8,128)(2,1)S(1)} custom-call(s32[1]{0:T(128)} %bitcast.8.view_ref, bf16[4,256,1536]{2,1,0:T(8,128)(2,1)S(1)} %copy-done.5, bf16[1536,3072]{1,0:T(8,128)(2,1)S(1)} %copy-done.1), custom_call_target="tpu_custom_call" | custom-call | flops 2415919104 | bytes 11010048 | tf_op jit(solution)/shard_map/pallas_call | solution.py:37
  22.2 6.3 %all-to-all-start = ((bf16[8,256,384]{2,1,0:T(8,128)(2,1)}), bf16[8,256,384]{2,1,0:T(8,128)(2,1)}, u32[]{:S(2)}, u32[]{:S(2)}) async-start(bf16[8,256,384]{2,1,0:T(8,128)(2,1)} %copy-done.12), calls=%async_computation | async-start | bytes 3145728 | tf_op jit(solution)/shard_map/all_to_all | solution.py:235
  28.6 3.7 copy-done.2
  32.2 1.9 copy-done.6
  34.1 6.7 %shard_map.73 = bf16[8,256,384]{2,1,0:T(8,128)(2,1)S(1)} custom-call(s32[1]{0:T(128)} %bitcast.7.view_ref, bf16[4,256,1536]{2,1,0:T(8,128)(2,1)S(1)} %copy-done.6, bf16[1536,3072]{1,0:T(8,128)(2,1)S(1)} %copy-done.2), custom_call_target="tpu_custom_call" | custom-call | flops 2415919104 | bytes 11010048 | tf_op jit(solution)/shard_map/pallas_call | solution.py:37
  42.0 24.5 %all-to-all-done = bf16[8,256,384]{2,1,0:T(8,128)(2,1)} async-done(((bf16[8,256,384]{2,1,0:T(8,128)(2,1)}), bf16[8,256,384]{2,1,0:T(8,128)(2,1)}, u32[]{:S(2)}, u32[]{:S(2)}) %all-to-all-start) | async-done | bytes 1572896 | tf_op jit(solution)/shard_map/all_to_all | solution.py:235
  66.5 4.3 %all-to-all-start.1 = ((bf16[8,256,384]{2,1,0:T(8,128)(2,1)}), bf16[8,256,384]{2,1,0:T(8,128)(2,1)}, u32[]{:S(2)}, u32[]{:S(2)}) async-start(bf16[8,256,384]{2,1,0:T(8,128)(2,1)} %copy-done.11), calls=%async_computation.1 | async-start | bytes 3145728 | tf_op jit(solution)/shard_map/all_to_all | solution.py:235
  70.8 3.7 copy-done.3
  74.5 1.9 copy-done.7
  76.4 6.6 %shard_map.76 = bf16[8,256,384]{2,1,0:T(8,128)(2,1)S(1)} custom-call(s32[1]{0:T(128)} %bitcast.10.view_ref, bf16[4,256,1536]{2,1,0:T(8,128)(2,1)S(1)} %copy-done.7, bf16[1536,3072]{1,0:T(8,128)(2,1)S(1)} %copy-done.3), custom_call_target="tpu_custom_call" | custom-call | flops 2415919104 | bytes 11010048 | tf_op jit(solution)/shard_map/pallas_call | solution.py:37
  84.1 24.5 %all-to-all-done.1 = bf16[8,256,384]{2,1,0:T(8,128)(2,1)} async-done(((bf16[8,256,384]{2,1,0:T(8,128)(2,1)}), bf16[8,256,384]{2,1,0:T(8,128)(2,1)}, u32[]{:S(2)}, u32[]{:S(2)}) %all-to-all-start.1) | async-done | bytes 1572896 | tf_op jit(solution)/shard_map/all_to_all | solution.py:235
  108.6 4.3 %all-to-all-start.2 = ((bf16[8,256,384]{2,1,0:T(8,128)(2,1)}), bf16[8,256,384]{2,1,0:T(8,128)(2,1)}, u32[]{:S(2)}, u32[]{:S(2)}) async-start(bf16[8,256,384]{2,1,0:T(8,128)(2,1)} %copy-done.10), calls=%async_computation.2 | async-start | bytes 3145728 | tf_op jit(solution)/shard_map/all_to_all | solution.py:235
  112.9 3.7 copy-done.4
  116.6 1.9 copy-done.8
  118.5 6.7 %shard_map.77 = bf16[8,256,384]{2,1,0:T(8,128)(2,1)S(1)} custom-call(s32[1]{0:T(128)} %bitcast.12.view_ref, bf16[4,256,1536]{2,1,0:T(8,128)(2,1)S(1)} %copy-done.8, bf16[1536,3072]{1,0:T(8,128)(2,1)S(1)} %copy-done.4), custom_call_target="tpu_custom_call" | custom-call | flops 2415919104 | bytes 11010048 | tf_op jit(solution)/shard_map/pallas_call | solution.py:37
  125.2 1.2 copy-done.9
  126.4 24.3 %all-to-all-done.2 = bf16[8,256,384]{2,1,0:T(8,128)(2,1)} async-done(((bf16[8,256,384]{2,1,0:T(8,128)(2,1)}), bf16[8,256,384]{2,1,0:T(8,128)(2,1)}, u32[]{:S(2)}, u32[]{:S(2)}) %all-to-all-start.2) | async-done | bytes 1572896 | tf_op jit(solution)/shard_map/all_to_all | solution.py:235
  150.8 4.3 %all-to-all-start.3 = ((bf16[8,256,384]{2,1,0:T(8,128)(2,1)}), bf16[8,256,384]{2,1,0:T(8,128)(2,1)}, u32[]{:S(2)}, u32[]{:S(2)}) async-start(bf16[8,256,384]{2,1,0:T(8,128)(2,1)} %copy-done.9), calls=%async_computation.3 | async-start | bytes 3145728 | tf_op jit(solution)/shard_map/all_to_all | solution.py:235
  158.4 3.8 %select_select_fusion = (bf16[2048,256]{1,0:T(8,128)(2,1)}, bf16[2048,256]{1,0:T(8,128)(2,1)}, bf16[2048,256]{1,0:T(8,128)(2,1)}) fusion(pred[]{:T(512)} %bitcast.18, pred[]{:T(512)} %bitcast.17, bf16[2048,384]{1,0:T(8,128)(2,1)} %bitcast.11.refs_1_.q_ref.own_k.own_v, bf16[2048,384]{1,0:T(8,128)(2,1)} %bitcast.13.refs_2_.q_ref.own_k.own_v, ...), kind=kLoop, calls=%fused_computation.16 | loop fusion | flops 2621440 | bytes 6291461 | tf_op jit(solution)/shard_map/jit(_where)/select_n | solution.py:225
  169.7 1.5 collective-permute-start
  171.3 1.4 collective-permute-start.1
  189.1 41.7 %all-reduce.2.cloned.1.call-done.anchor_k.anchor_v = bf16[2048,256]{1,0:T(8,128)(2,1)} async-done(((bf16[2048,256]{1,0:T(8,128)(2,1)}), bf16[2048,256]{1,0:T(8,128)(2,1)}) %all-reduce.2.cloned.1.call-update) | async-done | bytes 1048592 | tf_op jit(solution)/shard_map/psum | solution.py:21
  230.8 1.2 copy-done.21
  232.1 14.2 %shard_map.81 = (f32[2048,128]{1,0:T(8,128)S(1)}, f32[2048,128]{1,0:T(8,128)S(1)}) custom-call(bf16[2048,384]{1,0:T(8,128)(2,1)} %bitcast.13.refs_2_.q_ref.own_k.own_v, bf16[2048,384]{1,0:T(8,128)(2,1)} %bitcast.13.refs_2_.q_ref.own_k.own_v, bf16[2048,384]{1,0:T(8,128)(2,1)} %bitcast.13.refs_2_.q_ref.own_k.own_v, bf16[2048,256]{1,0:T(8,128)(2,1)S(1)} %copy-done.21, ...), custom_call_target="tpu_custom_call" | custom-call | flops 8589934592 | bytes 4718592 | tf_op jit(solution)/shard_map/pallas_call | solution.py:102
  248.3 1.2 copy-done.18
  249.5 1.2 copy-done.20
  250.7 6.8 %shard_map.82 = bf16[2048,128]{1,0:T(8,128)(2,1)S(1)} custom-call(s32[2]{0:T(128)S(1)} %get-tuple-element.56.pick_ref, s32[16,6]{1,0:T(8,128)S(1)} %bitcast.117, bf16[2048,384]{1,0:T(8,128)(2,1)} %bitcast.13.refs_2_.q_ref.own_k.own_v, f32[2048,128]{1,0:T(8,128)S(1)} %copy-done.18, f32[2048,128]{1,0:T(8,128)S(1)} %copy-done.20, ...), custom_call_target="tpu_custom_call" | custom-call | flops 1610612736 | bytes 5242880 | tf_op jit(solution)/shard_map/pallas_call | solution.py:177
  258.4 4.6 %all-to-all-start.6 = ((bf16[8,256,128]{2,1,0:T(8,128)(2,1)}), bf16[8,256,128]{2,1,0:T(8,128)(2,1)}, u32[]{:S(2)}, u32[]{:S(2)}) async-start(bf16[8,256,128]{2,1,0:T(8,128)(2,1)} %bitcast.113), calls=%async_computation.6 | async-start | bytes 1048576 | tf_op jit(solution)/shard_map/all_to_all | solution.py:266
  263.0 1.2 copy-done.22
  264.2 14.2 %shard_map.79 = (f32[2048,128]{1,0:T(8,128)S(1)}, f32[2048,128]{1,0:T(8,128)S(1)}) custom-call(bf16[2048,384]{1,0:T(8,128)(2,1)} %bitcast.11.refs_1_.q_ref.own_k.own_v, bf16[2048,384]{1,0:T(8,128)(2,1)} %bitcast.11.refs_1_.q_ref.own_k.own_v, bf16[2048,384]{1,0:T(8,128)(2,1)} %bitcast.11.refs_1_.q_ref.own_k.own_v, bf16[2048,256]{1,0:T(8,128)(2,1)S(1)} %copy-done.22, ...), custom_call_target="tpu_custom_call" | custom-call | flops 8589934592 | bytes 4718592 | tf_op jit(solution)/shard_map/pallas_call | solution.py:102
  278.4 6.9 %shard_map.80 = bf16[2048,128]{1,0:T(8,128)(2,1)S(1)} custom-call(s32[2]{0:T(128)S(1)} %get-tuple-element.55.pick_ref, s32[16,6]{1,0:T(8,128)S(1)} %bitcast.116, bf16[2048,384]{1,0:T(8,128)(2,1)} %bitcast.11.refs_1_.q_ref.own_k.own_v, f32[2048,128]{1,0:T(8,128)S(1)} %get-tuple-element.27.sum_ref, f32[2048,128]{1,0:T(8,128)S(1)} %get-tuple-element.28.stat_ref, ...), custom_call_target="tpu_custom_call" | custom-call | flops 1610612736 | bytes 5242880 | tf_op jit(solution)/shard_map/pallas_call | solution.py:177
  286.1 5.1 %all-to-all-start.5 = ((bf16[8,256,128]{2,1,0:T(8,128)(2,1)}), bf16[8,256,128]{2,1,0:T(8,128)(2,1)}, u32[]{:S(2)}, u32[]{:S(2)}) async-start(bf16[8,256,128]{2,1,0:T(8,128)(2,1)} %bitcast.112), calls=%async_computation.5 | async-start | bytes 1048576 | tf_op jit(solution)/shard_map/all_to_all | solution.py:266
  291.2 1.2 copy-done.23
  292.4 14.2 %shard_map.75 = (f32[2048,128]{1,0:T(8,128)S(1)}, f32[2048,128]{1,0:T(8,128)S(1)}) custom-call(bf16[2048,384]{1,0:T(8,128)(2,1)} %bitcast.9.q_ref.own_k.own_v.refs_0_, bf16[2048,384]{1,0:T(8,128)(2,1)} %bitcast.9.q_ref.own_k.own_v.refs_0_, bf16[2048,384]{1,0:T(8,128)(2,1)} %bitcast.9.q_ref.own_k.own_v.refs_0_, bf16[2048,256]{1,0:T(8,128)(2,1)S(1)} %copy-done.23, ...), custom_call_target="tpu_custom_call" | custom-call | flops 8589934592 | bytes 4718592 | tf_op jit(solution)/shard_map/pallas_call | solution.py:102
  306.6 6.9 %shard_map.78 = bf16[2048,128]{1,0:T(8,128)(2,1)S(1)} custom-call(s32[2]{0:T(128)S(1)} %get-tuple-element.54.pick_ref, s32[16,6]{1,0:T(8,128)S(1)} %bitcast.115, bf16[2048,384]{1,0:T(8,128)(2,1)} %bitcast.9.q_ref.own_k.own_v.refs_0_, f32[2048,128]{1,0:T(8,128)S(1)} %get-tuple-element.20.sum_ref, f32[2048,128]{1,0:T(8,128)S(1)} %get-tuple-element.21.stat_ref, ...), custom_call_target="tpu_custom_call" | custom-call | flops 1610612736 | bytes 5242880 | tf_op jit(solution)/shard_map/pallas_call | solution.py:177
  314.3 5.1 %all-to-all-start.4 = ((bf16[8,256,128]{2,1,0:T(8,128)(2,1)}), bf16[8,256,128]{2,1,0:T(8,128)(2,1)}, u32[]{:S(2)}, u32[]{:S(2)}) async-start(bf16[8,256,128]{2,1,0:T(8,128)(2,1)} %bitcast.111), calls=%async_computation.4 | async-start | bytes 1048576 | tf_op jit(solution)/shard_map/all_to_all | solution.py:266
  319.4 1.2 copy-done.24
  320.7 14.2 %shard_map.83 = (f32[2048,128]{1,0:T(8,128)S(1)}, f32[2048,128]{1,0:T(8,128)S(1)}) custom-call(bf16[2048,384]{1,0:T(8,128)(2,1)} %bitcast.14.refs_3_.q_ref.own_k.own_v, bf16[2048,384]{1,0:T(8,128)(2,1)} %bitcast.14.refs_3_.q_ref.own_k.own_v, bf16[2048,384]{1,0:T(8,128)(2,1)} %bitcast.14.refs_3_.q_ref.own_k.own_v, bf16[2048,256]{1,0:T(8,128)(2,1)S(1)} %copy-done.24, ...), custom_call_target="tpu_custom_call" | custom-call | flops 8589934592 | bytes 4718592 | tf_op jit(solution)/shard_map/pallas_call | solution.py:102
  334.8 6.9 %shard_map.84 = bf16[2048,128]{1,0:T(8,128)(2,1)S(1)} custom-call(s32[2]{0:T(128)S(1)} %get-tuple-element.57.pick_ref, s32[16,6]{1,0:T(8,128)S(1)} %bitcast.114, bf16[2048,384]{1,0:T(8,128)(2,1)} %bitcast.14.refs_3_.q_ref.own_k.own_v, f32[2048,128]{1,0:T(8,128)S(1)} %get-tuple-element.31.sum_ref, f32[2048,128]{1,0:T(8,128)S(1)} %get-tuple-element.32.stat_ref, ...), custom_call_target="tpu_custom_call" | custom-call | flops 1610612736 | bytes 5242880 | tf_op jit(solution)/shard_map/pallas_call | solution.py:177
  342.5 5.1 %all-to-all-start.7 = ((bf16[8,256,128]{2,1,0:T(8,128)(2,1)}), bf16[8,256,128]{2,1,0:T(8,128)(2,1)}, u32[]{:S(2)}, u32[]{:S(2)}) async-start(bf16[8,256,128]{2,1,0:T(8,128)(2,1)} %bitcast.110), calls=%async_computation.7 | async-start | bytes 1048576 | tf_op jit(solution)/shard_map/all_to_all | solution.py:266
  347.6 1.9 broadcast_in_dim.19
  349.5 2.9 fusion.11
  352.4 2.9 fusion.9
  355.3 2.9 fusion.7
  358.2 4.9 %all-to-all-done.7 = bf16[8,256,128]{2,1,0:T(8,128)(2,1)} async-done(((bf16[8,256,128]{2,1,0:T(8,128)(2,1)}), bf16[8,256,128]{2,1,0:T(8,128)(2,1)}, u32[]{:S(2)}, u32[]{:S(2)}) %all-to-all-start.7) | async-done | bytes 524320 | tf_op jit(solution)/shard_map/all_to_all | solution.py:266
  363.1 2.9 fusion.5
  (59 shorter events, 12.1 us)
Async XLA Ops:
  6.5 341.1 %copy-start = (bf16[1024,1536]{1,0:T(8,128)(2,1)S(1)}, bf16[1024,1536]{1,0:T(8,128)(2,1)}, u32[]{:S(2)}) copy-start(bf16[1024,1536]{1,0:T(8,128)(2,1)} %param.9) | copy-start | bytes 9437188
  8.9 3.7 copy-start.1
  12.5 1.9 copy-start.5
  21.1 1.1 copy-start.12
  22.2 44.3 %all-to-all-start = ((bf16[8,256,384]{2,1,0:T(8,128)(2,1)}), bf16[8,256,384]{2,1,0:T(8,128)(2,1)}, u32[]{:S(2)}, u32[]{:S(2)}) async-start(bf16[8,256,384]{2,1,0:T(8,128)(2,1)} %copy-done.12), calls=%async_computation | async-start | bytes 3145728 | tf_op jit(solution)/shard_map/all_to_all | solution.py:235
  28.6 3.7 copy-start.2
  32.2 1.9 copy-start.6
  40.8 1.2 copy-start.11
  66.5 42.1 %all-to-all-start.1 = ((bf16[8,256,384]{2,1,0:T(8,128)(2,1)}), bf16[8,256,384]{2,1,0:T(8,128)(2,1)}, u32[]{:S(2)}, u32[]{:S(2)}) async-start(bf16[8,256,384]{2,1,0:T(8,128)(2,1)} %copy-done.11), calls=%async_computation.1 | async-start | bytes 3145728 | tf_op jit(solution)/shard_map/all_to_all | solution.py:235
  70.8 3.7 copy-start.3
  74.5 1.9 copy-start.7
  83.0 1.1 copy-start.10
  108.6 42.1 %all-to-all-start.2 = ((bf16[8,256,384]{2,1,0:T(8,128)(2,1)}), bf16[8,256,384]{2,1,0:T(8,128)(2,1)}, u32[]{:S(2)}, u32[]{:S(2)}) async-start(bf16[8,256,384]{2,1,0:T(8,128)(2,1)} %copy-done.10), calls=%async_computation.2 | async-start | bytes 3145728 | tf_op jit(solution)/shard_map/all_to_all | solution.py:235
  112.9 3.7 copy-start.4
  116.6 1.9 copy-start.8
  125.2 1.2 copy-start.9
  126.4 28.7 %copy-start.26 = (s32[4,4]{1,0:T(4,128)S(1)}, s32[4,4]{1,0:T(4,128)}, u32[]{:S(2)}) copy-start(s32[4,4]{1,0:T(4,128)} %constant.188.clone) | copy-start | bytes 196
  150.8 97.5 %all-to-all-start.3 = ((bf16[8,256,384]{2,1,0:T(8,128)(2,1)}), bf16[8,256,384]{2,1,0:T(8,128)(2,1)}, u32[]{:S(2)}, u32[]{:S(2)}) async-start(bf16[8,256,384]{2,1,0:T(8,128)(2,1)} %copy-done.9), calls=%async_computation.3 | async-start | bytes 3145728 | tf_op jit(solution)/shard_map/all_to_all | solution.py:235
  155.1 75.8 %all-reduce.2.cloned.1.call-start = ((), (), s32[]{:S(2)}) async-start(), calls=%async_computation.8 | async-start | bytes 2097152 | tf_op jit(solution)/shard_map/psum | solution.py:21
  158.4 14.3 %copy-start.25 = (s32[4,16,6]{1,0,2:T(4,128)S(1)}, s32[4,16,6]{1,0,2:T(4,128)}, u32[]{:S(2)}) copy-start(s32[4,16,6]{1,0,2:T(4,128)} %param.11) | copy-start | bytes 4612
  169.7 78.5 %collective-permute-start = (bf16[2048,256]{1,0:T(8,128)(2,1)}, bf16[2048,256]{1,0:T(8,128)(2,1)}, u32[]{:S(2)}, u32[]{:S(2)}) collective-permute-start(bf16[2048,256]{1,0:T(8,128)(2,1)} %get-tuple-element.34), channel_id=1, source_target_pairs={{0,8},{8,16},{16,24},{24,0},{1,9},{9,17},{17,25},{25,1},{2,10},{10... | collective-permute-start | bytes 3145736 | tf_op jit(solution)/shard_map/ppermute | solution.py:26
  171.3 77.0 %collective-permute-start.1 = (bf16[2048,256]{1,0:T(8,128)(2,1)}, bf16[2048,256]{1,0:T(8,128)(2,1)}, u32[]{:S(2)}, u32[]{:S(2)}) collective-permute-start(bf16[2048,256]{1,0:T(8,128)(2,1)} %get-tuple-element.33), channel_id=1, source_target_pairs={{0,24},{8,0},{16,8},{24,16},{1,25},{9,1},{17,9},{25,17},{2,26},{10... | collective-permute-start | bytes 3145736 | tf_op jit(solution)/shard_map/ppermute | solution.py:26
  230.8 1.2 copy-start.21
  246.2 1.0 copy-start.17
  247.3 1.0 copy-start.19
  248.3 1.2 copy-start.18
  249.5 1.2 copy-start.20
  257.6 0.8 copy-start.16
  258.4 27.7 %all-to-all-start.6 = ((bf16[8,256,128]{2,1,0:T(8,128)(2,1)}), bf16[8,256,128]{2,1,0:T(8,128)(2,1)}, u32[]{:S(2)}, u32[]{:S(2)}) async-start(bf16[8,256,128]{2,1,0:T(8,128)(2,1)} %bitcast.113), calls=%async_computation.6 | async-start | bytes 1048576 | tf_op jit(solution)/shard_map/all_to_all | solution.py:266
  263.0 1.2 copy-start.22
  285.3 0.8 copy-start.15
  286.1 28.2 %all-to-all-start.5 = ((bf16[8,256,128]{2,1,0:T(8,128)(2,1)}), bf16[8,256,128]{2,1,0:T(8,128)(2,1)}, u32[]{:S(2)}, u32[]{:S(2)}) async-start(bf16[8,256,128]{2,1,0:T(8,128)(2,1)} %bitcast.112), calls=%async_computation.5 | async-start | bytes 1048576 | tf_op jit(solution)/shard_map/all_to_all | solution.py:266
  291.2 1.2 copy-start.23
  313.5 0.8 copy-start.14
  314.3 28.2 %all-to-all-start.4 = ((bf16[8,256,128]{2,1,0:T(8,128)(2,1)}), bf16[8,256,128]{2,1,0:T(8,128)(2,1)}, u32[]{:S(2)}, u32[]{:S(2)}) async-start(bf16[8,256,128]{2,1,0:T(8,128)(2,1)} %bitcast.111), calls=%async_computation.4 | async-start | bytes 1048576 | tf_op jit(solution)/shard_map/all_to_all | solution.py:266
  319.4 1.2 copy-start.24
  341.7 0.8 copy-start.13
  342.5 20.6 %all-to-all-start.7 = ((bf16[8,256,128]{2,1,0:T(8,128)(2,1)}), bf16[8,256,128]{2,1,0:T(8,128)(2,1)}, u32[]{:S(2)}, u32[]{:S(2)}) async-start(bf16[8,256,128]{2,1,0:T(8,128)(2,1)} %bitcast.110), calls=%async_computation.7 | async-start | bytes 1048576 | tf_op jit(solution)/shard_map/all_to_all | solution.py:266
Sparse Core Ops, SparseCore 0:
  162.3 68.4 all-reduce.1
